TPU v7x, 32 devices: a whole 2x2x4 slice. The times are simulated.
32 devices in a mesh: island: 16 (over z, y, x), fsdp: 2 (over core).
Axes of the slice: x: 2, y: 2, z: 4, core: 2. Of those that a mesh axis runs over, the one named last changes fastest.
Arguments:
- global_weights: float32 [4, 64, 8192], P(None, 'fsdp'), may hold values from -6 to 6
- local_weights: float32 [16, 4, 64, 8192], P('island', None, 'fsdp'), may hold values from -6 to 6
- momentum: float32 [4, 64, 8192], P(None, 'fsdp', 'island'), may hold values from -4 to 4
Outputs:
- new_global: float32 [4, 64, 8192], P(None, 'fsdp')
- new_momentum: float32 [4, 64, 8192], P(None, 'fsdp', 'island')
All inputs are finite; a program needn't handle non-finite values.
Results may differ from a plain program's by a relative error of at most 0.00002.
Values sent between devices are 32-bit elements; how exact they have to be, the bound alone decides.
A program may use at most 64 MiB of HBM per device.

v0:
```python
import jax
from jax import lax
from jax.sharding import PartitionSpec as P

NESTEROV = 0.9
OUTER_RATE = 0.7


def body(global_weights, local_weights, momentum):
    pseudo_grad = global_weights - local_weights[0]
    islands_count = lax.axis_size("island")
    slice_cols = momentum.shape[2]
    offset = lax.axis_index("island") * slice_cols
    summed = lax.psum(pseudo_grad, "island")
    whole_moment = lax.all_gather(momentum, "island", axis=2, tiled=True)
    outer_grad = summed / islands_count
    moment_all = NESTEROV * whole_moment + outer_grad
    new_global = global_weights - OUTER_RATE * (outer_grad + NESTEROV * moment_all)
    new_momentum = lax.dynamic_slice_in_dim(moment_all, offset, slice_cols, 2)
    return (new_global, new_momentum)


def solution(mesh):
    return jax.shard_map(
        body,
        mesh=mesh,
        in_specs=(
            P(None, "fsdp", None),
            P("island", None, "fsdp", None),
            P(None, "fsdp", "island"),
        ),
        out_specs=(P(None, "fsdp", None), P(None, "fsdp", "island")),
        check_vma=False,
    )
```

profile of v0, /device:TPU:0, one launch (start us, length us, event | category | flops | bytes accessed | tf_op | source)
XLA Modules:
  0.0 279.2 jit_solution(9286125899146317759)
XLA Ops:
  7.2 0.0 all-reduce.2.cloned.1.call-start
  7.2 6.0 %bitcast_subtract_fusion = f32[4,32,8192]{2,1,0:T(8,128)} fusion(f32[4,32,8192]{2,1,0:T(8,128)} %param.3, f32[1,4,32,8192]{3,2,1,0:T(8,128)} %param.4), kind=kLoop, calls=%fused_computation | loop fusion | flops 1048576 | bytes 12582912 | tf_op jit(solution)/shard_map/sub | solution.py:10
  13.2 0.0 all-reduce.2.cloned.1.call-update
  13.2 0.0 all-gather.2.cloned.1.call-start
  13.3 0.7 all-gather.2.cloned.1.call-update
  14.0 171.1 %all-reduce.2.cloned.1.call-done = f32[4,32,8192]{2,1,0:T(8,128)} async-done(((f32[4,32,8192]{2,1,0:T(8,128)}), f32[4,32,8192]{2,1,0:T(8,128)}) %all-reduce.2.cloned.1.call-update) | async-done | bytes 4194320 | tf_op jit(solution)/shard_map/psum | solution.py:14
  185.1 78.5 %all-gather.2.cloned.1.call-done = f32[4,32,8192]{2,1,0:T(8,128)} async-done(((f32[4,32,512]{2,1,0:T(8,128)}), f32[4,32,8192]{2,1,0:T(8,128)}) %all-gather.2.cloned.1.call-update) | async-done | bytes 4194320 | tf_op jit(solution)/shard_map/all_gather | solution.py:15
  263.6 8.1 %multiply_add_fusion = (f32[4,32,8192]{2,1,0:T(8,128)S(1)}, f32[4,32,8192]{2,1,0:T(8,128)}) fusion(f32[4,32,8192]{2,1,0:T(8,128)} %all-gather.2.cloned.1.call-done, f32[4,32,8192]{2,1,0:T(8,128)} %all-reduce.2.cloned.1.call-done, f32[4,32,8192]{2,1,0:T(8,128)} %param.3), kind=kLoop, calls=%fused_computation.2 | loop fusion | flops 7340032 | bytes 20971520 | tf_op jit(solution)/shard_map/add | solution.py:17
  271.7 0.7 constant_dynamic-slice_fusion
Async XLA Ops:
  7.2 177.9 %all-reduce.2.cloned.1.call-start = ((), (), s32[]{:S(2)}) async-start(), calls=%async_computation | async-start | bytes 8388608 | tf_op jit(solution)/shard_map/psum | solution.py:14
  13.2 250.4 %all-gather.2.cloned.1.call-start = ((), (), s32[]{:S(2)}) async-start(), calls=%async_computation.1 | async-start | bytes 4456448 | tf_op jit(solution)/shard_map/all_gather | solution.py:15
Sparse Core Ops, SparseCore 0:
  14.2 170.8 all-reduce.1
  188.2 75.3 all-gather.1
where the time goes:
time: 279 us
  waiting for transfers between devices  250 us (90%)
  other arithmetic  14.1 us (5%)
  between operations  14 us (5%)
    psum x1, waiting for transfers between devices, body(): summed = lax.psum(pseudo_grad, 'island')  171 us
    all_gather x1, waiting for transfers between devices, body(): whole_moment = lax.all_gather(momentum, 'island', axis=2, tiled=True)  78.5 us
    add x1, other arithmetic, body(): moment_all = NESTEROV * whole_moment + outer_grad  8.07 us
    sub x1, other arithmetic, body(): pseudo_grad = global_weights - local_weights[0]  6 us
  transfers between devices with their start and end apart: 2, of which 2 were waited for; matrix products, arithmetic and copies ran while one was open for 0% of the time, Pallas kernels for 0%

commit v1 on v0

v1 whole, which is shorter than its diff:
```python
import functools

import jax
import jax.numpy as jnp
from jax import lax
from jax.experimental import pallas as pl
from jax.experimental.pallas import tpu as pltpu
from jax.sharding import PartitionSpec as P

NESTEROV = 0.9
OUTER_RATE = 0.7
LANES = 128
SUBLANES = 8


def grid_of(islands):
    return {16: (4, 2, 2), 64: (8, 8)}.get(islands, (islands,))


def plan(dims, groups):
    if len(dims) == 3:
        z, y, x = 0, 1, 2
        wish = [((z, y, x), 2), ((x, y, z), 3), ((y, x, z), 3),
                ((z, x, y), 2), ((x, y, z), 2), ((y, x, z), 2), ((z, y, x), 2)]
    elif len(dims) == 2:
        wish = [((0, 1), 1), ((1, 0), 1)]
    else:
        wish = [((0,), 1)]
    total = sum(share for _, share in wish)
    streams, at, seen = [], 0, 0
    for order, share in wish:
        seen += share
        end = groups * seen // total
        if end > at:
            streams.append((order, at, end - at))
        at = end
    return streams


def phase_slots(n):
    return 1 if n == 2 else 2 * (n - 1)


def kernel(dims, streams, n_sems, g_hbm, l_hbm, m_hbm, out_hbm, nm_hbm,
           gw, lw, mom, acc, gath, nm, landing, send_sem, recv_sem, in_sem, out_sem):
    axes = range(len(dims))
    me = lax.axis_index("island")
    strides = []
    for a in axes:
        stride = 1
        for b in dims[a + 1:]:
            stride *= b
        strides.append(stride)
    pos = [(me // strides[a]) % dims[a] for a in axes]
    islands = strides[0] * dims[0]

    loads = []
    for j, (_, g0, ng) in enumerate(streams):
        rows = pl.ds(g0, ng)
        loads.append([
            pltpu.make_async_copy(g_hbm.at[rows], gw.at[rows], in_sem.at[3 * j]),
            pltpu.make_async_copy(l_hbm.at[rows], lw.at[rows], in_sem.at[3 * j + 1]),
            pltpu.make_async_copy(m_hbm.at[rows], mom.at[rows], in_sem.at[3 * j + 2]),
        ])
        for load in loads[-1][:2]:
            load.start()
    for load in loads:
        load[2].start()

    barrier = pltpu.get_barrier_semaphore()
    for a in axes:
        for step, there in ((1, pos[a] < dims[a] - 1), (-1, pos[a] > 0)):
            @pl.when(there)
            def _():
                pl.semaphore_signal(barrier, inc=1,
                                    device_id={"island": me + step * strides[a]},
                                    device_id_type=pl.DeviceIdType.MESH)

    counter = iter(range(n_sems))
    ends = []

    def remote(src, dst, sem, axis, step):
        return pltpu.make_async_remote_copy(
            src_ref=src, dst_ref=dst, send_sem=send_sem.at[sem],
            recv_sem=recv_sem.at[sem],
            device_id={"island": me + step * strides[axis]},
            device_id_type=pl.DeviceIdType.MESH)

    def part(ref, rows, fixed):
        return ref.at[(rows,) + tuple(fixed.get(a, slice(None)) for a in axes)]

    def stream(j):
        order, g0, ng = streams[j]
        rows = pl.ds(g0, ng)
        loads[j][0].wait()
        loads[j][1].wait()
        acc[rows] = gw[rows] - lw[rows]
        yield
        fixed = {}
        for phase, a in enumerate(order):
            n, p = dims[a], pos[a]
            land = landing[j * len(dims) + phase]
            sems = [[next(counter) for _ in range(n - 1)] for _ in range(2)]

            def slot(side, k, land=land, n=n):
                return land.at[0 if n == 2 else side * (n - 1) + k]

            def mine(s, a=a, fixed=dict(fixed)):
                return part(acc, rows, {**fixed, a: s})

            def take(side, k, s):
                block = mine(s)
                remote(block, slot(side, k), sems[side][k], a, 1 - 2 * side).wait_recv()
                block[...] = block[...] + slot(side, k)[...]

            for k in range(n - 1):
                for side in range(2):
                    lead = p if side == 0 else n - 1 - p
                    s = n - 1 - k + p if side == 0 else k - lead

                    @pl.when(lead <= k)
                    def _():
                        if k > 0:
                            @pl.when(lead > 0)
                            def _():
                                take(side, k - 1, s)
                        remote(mine(s), slot(side, k), sems[side][k], a,
                               1 - 2 * side).start()

                    def end(lead=lead, k=k, side=side, s=s, a=a,
                            mine=mine, slot=slot, sems=sems):
                        @pl.when(lead <= k)
                        def _():
                            remote(mine(s), slot(side, k), sems[side][k], a,
                                   1 - 2 * side).wait_send()
                    ends.append(end)
                yield
            for side in range(2):
                @pl.when((p if side == 0 else n - 1 - p) > 0)
                def _():
                    take(side, n - 2, p)
            fixed[a] = p

        own = (rows,) + tuple(pos)
        loads[j][2].wait()
        outer = acc[own] / islands
        moment = NESTEROV * mom[rows] + outer
        nm[rows] = moment
        gath[own] = gw[own] - OUTER_RATE * (outer + NESTEROV * moment)
        save = pltpu.make_async_copy(nm.at[rows], nm_hbm.at[rows], out_sem.at[2 * j])
        save.start()
        ends.append(save.wait)

        for a in reversed(order):
            n, p = dims[a], pos[a]
            del fixed[a]
            sems = [[next(counter) for _ in range(n - 1)] for _ in range(2)]

            def block_of(s, a=a, fixed=dict(fixed)):
                return part(gath, rows, {**fixed, a: s})

            for k in range(n):
                for side in range(2):
                    step = 1 - 2 * side
                    lead = p if side == 0 else n - 1 - p
                    s = p - step * k

                    @pl.when(k <= lead)
                    def _():
                        block = block_of(s)
                        if k > 0:
                            remote(block, block, sems[side][k - 1], a, step).wait_recv()
                        if k < n - 1:
                            @pl.when(lead < n - 1)
                            def _():
                                remote(block, block, sems[side][k], a, step).start()

                    if k < n - 1:
                        def end(k=k, lead=lead, n=n, s=s, side=side, step=step, a=a,
                                block_of=block_of, sems=sems):
                            @pl.when((k <= lead) & (lead < n - 1))
                            def _():
                                block = block_of(s)
                                remote(block, block, sems[side][k], a, step).wait_send()
                        ends.append(end)
                if k < n - 1:
                    yield
        store = pltpu.make_async_copy(gath.at[rows], out_hbm.at[rows], out_sem.at[2 * j + 1])
        store.start()
        ends.append(store.wait)

    running = [stream(j) for j in range(len(streams))]
    first = True
    while running:
        for one in list(running):
            if next(one, "end") == "end":
                running.remove(one)
            elif first:
                first = False
                peers = sum((pos[a] < dims[a] - 1).astype(jnp.int32)
                            + (pos[a] > 0).astype(jnp.int32) for a in axes)
                pl.semaphore_wait(barrier, peers)
    for end in ends:
        end()


def body(dims, global_weights, local_weights, momentum):
    layers, rows, width = global_weights.shape
    islands = lax.axis_size("island")
    cols = momentum.shape[2]
    groups = layers * rows // SUBLANES
    tiles = cols // LANES

    def to_tiles(array):
        array = array.reshape(groups, SUBLANES, -1, LANES)
        return array.transpose(0, 2, 1, 3)

    def from_tiles(array, like):
        array = array.reshape(groups, -1, SUBLANES, LANES)
        return array.transpose(0, 2, 1, 3).reshape(like.shape)

    wide = (groups,) + dims + (tiles, SUBLANES, LANES)
    narrow = (groups, tiles, SUBLANES, LANES)
    streams = plan(dims, groups)
    landings = []
    for order, _, ng in streams:
        left = dict(enumerate(dims))
        for a in order:
            n = left.pop(a)
            landings.append(pltpu.VMEM(
                (phase_slots(n), ng) + tuple(left[b] for b in sorted(left))
                + (tiles, SUBLANES, LANES), jnp.float32))
    n_sems = len(streams) * 4 * sum(n - 1 for n in dims)
    f32 = jnp.float32
    new_global, new_momentum = pl.pallas_call(
        functools.partial(kernel, dims, streams, n_sems),
        out_shape=(jax.ShapeDtypeStruct(wide, f32), jax.ShapeDtypeStruct(narrow, f32)),
        in_specs=[pl.BlockSpec(memory_space=pl.ANY)] * 3,
        out_specs=(pl.BlockSpec(memory_space=pl.ANY),) * 2,
        scratch_shapes=[
            pltpu.VMEM(wide, f32), pltpu.VMEM(wide, f32), pltpu.VMEM(narrow, f32),
            pltpu.VMEM(wide, f32), pltpu.VMEM(wide, f32), pltpu.VMEM(narrow, f32),
            landings,
            pltpu.SemaphoreType.DMA((n_sems,)), pltpu.SemaphoreType.DMA((n_sems,)),
            pltpu.SemaphoreType.DMA((3 * len(streams),)),
            pltpu.SemaphoreType.DMA((2 * len(streams),)),
        ],
        compiler_params=pltpu.CompilerParams(
            collective_id=0, has_side_effects=True, vmem_limit_bytes=40 * 2**20),
    )(
        to_tiles(global_weights).reshape(wide),
        to_tiles(local_weights[0]).reshape(wide),
        to_tiles(momentum),
    )
    return from_tiles(new_global, global_weights), from_tiles(new_momentum, momentum)


def solution(mesh):
    dims = grid_of(mesh.shape["island"])
    return jax.shard_map(
        functools.partial(body, dims),
        mesh=mesh,
        in_specs=(
            P(None, "fsdp", None),
            P("island", None, "fsdp", None),
            P(None, "fsdp", "island"),
        ),
        out_specs=(P(None, "fsdp", None), P(None, "fsdp", "island")),
        check_vma=False,
    )
```

time: 279 us -> 92.1 us (0.33)
  waiting for transfers between devices: 250 us -> 0 us
  Pallas kernels: 0 us -> 83.2 us
  other arithmetic: 14.1 us -> 0 us
  between operations: 14 us -> 0.65 us
  local copies, waits for them, and re-layouts: 0.72 us -> 8.04 us
    psum x1 -> x0, waiting for transfers between devices: 171 us -> none  [body(): summed = lax.psum(pseudo_grad, 'island')]
    pallas_call x0 -> x1, Pallas kernels: none -> 83.2 us  [body(): pl.pallas_call(functools.partial(kernel, dims, streams, n_sems), out_shap...]
    all_gather x1 -> x0, waiting for transfers between devices: 78.5 us -> none  [body(): whole_moment = lax.all_gather(momentum, 'island', axis=2, tiled=True)]
    add x1 -> x0, other arithmetic: 8.07 us -> none  [body(): moment_all = NESTEROV * whole_moment + outer_grad]
    unnamed x0 -> x8, local copies, waits for them, and re-layouts: none -> 8.04 us
    sub x1 -> x0, other arithmetic: 6 us -> none  [body(): pseudo_grad = global_weights - local_weights[0]]
  transfers between devices with their start and end apart: 2 -> 0, of which waited for: 2 -> 0; matrix products, arithmetic and copies ran while one was open for 0% -> 0% of each run, Pallas kernels for 0% -> 0%
where the time goes in v1:
time: 92.1 us; the launch traced here: 91.9 us
  Pallas kernels  83.2 us (90%)
  local copies, waits for them, and re-layouts  8.04 us (9%)
    pallas_call x1, Pallas kernels, body(): pl.pallas_call(functools.partial(kernel, dims, streams, n_sems), out_shap...  83.2 us
    unnamed x8, local copies, waits for them, and re-layouts  8.04 us

profile of v1, /device:TPU:0, one launch (start us, length us, event | category | flops | bytes accessed | tf_op | source)
XLA Modules:
  0.0 91.9 jit_solution(7854351900532379906)
XLA Ops:
  0.6 0.0 copy-start
  0.6 2.2 %copy-done = f32[4,32,8192]{2,1,0:T(8,128)S(1)} copy-done((f32[4,32,8192]{2,1,0:T(8,128)S(1)}, f32[4,32,8192]{2,1,0:T(8,128)}, u32[]{:S(2)}) %copy-start) | copy-done | bytes 4194328
  2.8 0.0 copy-start.1
  2.8 2.2 %copy-done.1 = f32[1,4,32,8192]{3,2,1,0:T(8,128)S(1)} copy-done((f32[1,4,32,8192]{3,2,1,0:T(8,128)S(1)}, f32[1,4,32,8192]{3,2,1,0:T(8,128)}, u32[]{:S(2)}) %copy-start.1) | copy-done | bytes 4194328
  5.0 0.0 copy-start.2
  5.0 0.9 %copy-done.2 = f32[4,32,512]{2,1,0:T(8,128)S(1)} copy-done((f32[4,32,512]{2,1,0:T(8,128)S(1)}, f32[4,32,512]{2,1,0:T(8,128)}, u32[]{:S(2)}) %copy-start.2) | copy-done | bytes 262168
  6.0 83.2 %shard_map.50 = (f32[16,4,2,2,4,8,128]{6,5,4,3,2,1,0:T(8,128)S(1)}, f32[16,4,8,128]{3,2,1,0:T(8,128)S(1)}) custom-call(f32[16,4,2,2,4,8,128]{6,5,4,3,2,1,0:T(8,128)S(1)} %bitcast.21, f32[16,4,2,2,4,8,128]{6,5,4,3,2,1,0:T(8,128)S(1)} %bitcast.22, f32[16,4,8,128]{3,2,1,0:T(8,128)S(1)} %bitcast.24), custom_call_target="tpu_custom_call" | custom-call | tf_op jit(solution)/shard_map/pallas_call | solution.py:235
  89.2 2.0 %copy.7 = f32[4,32,8192]{2,1,0:T(8,128)} copy(f32[4,32,8192]{2,1,0:T(8,128)S(1)} %bitcast.23) | data formatting | bytes 8388608
  91.2 0.7 copy.8
Async XLA Ops:
  0.6 2.2 %copy-start = (f32[4,32,8192]{2,1,0:T(8,128)S(1)}, f32[4,32,8192]{2,1,0:T(8,128)}, u32[]{:S(2)}) copy-start(f32[4,32,8192]{2,1,0:T(8,128)} %param.3) | copy-start | bytes 12582916
  2.8 2.2 %copy-start.1 = (f32[1,4,32,8192]{3,2,1,0:T(8,128)S(1)}, f32[1,4,32,8192]{3,2,1,0:T(8,128)}, u32[]{:S(2)}) copy-start(f32[1,4,32,8192]{3,2,1,0:T(8,128)} %param.4) | copy-start | bytes 12582916
  5.0 0.9 %copy-start.2 = (f32[4,32,512]{2,1,0:T(8,128)S(1)}, f32[4,32,512]{2,1,0:T(8,128)}, u32[]{:S(2)}) copy-start(f32[4,32,512]{2,1,0:T(8,128)} %param.5) | copy-start | bytes 786436

commit v2 on v1

--- a/solution.py
+++ b/solution.py
@@ -9,6 +9,7 @@
 
 NESTEROV = 0.9
 OUTER_RATE = 0.7
+ORDER = [2, 2, 1, 1, 0, 3, 3, 5, 3, 0, 3, 0, 4, 0, 3, 2, 1, 5, 3, 4, 3, 0, 0, 2, 1, 2, 0, 3, 2, 1, 1, 2, 0, 1, 2, 2, 4, 5, 1, 1, 2, 2, 1, 1, 2, 2, 1, 0, 1, 4, 2, 5, 2, 4, 5, 3, 1, 1, 0, 4, 3, 2, 4, 1, 5, 5, 4, 4, 5, 5, 0, 3, 4, 4, 5, 5, 4, 1, 2, 4, 5, 4, 5, 3, 3, 5, 5, 0, 3, 5, 4, 4, 0, 3, 1, 3, 3, 5, 4, 0, 0, 0, 0, 2, 0, 3, 5, 4]
 LANES = 128
 SUBLANES = 8
 
@@ -20,8 +21,7 @@
 def plan(dims, groups):
     if len(dims) == 3:
         z, y, x = 0, 1, 2
-        wish = [((z, y, x), 2), ((x, y, z), 3), ((y, x, z), 3),
-                ((z, x, y), 2), ((x, y, z), 2), ((y, x, z), 2), ((z, y, x), 2)]
+        wish = [((0, 1, 2), 2), ((2, 1, 0), 3), ((1, 2, 0), 3), ((0, 2, 1), 2), ((2, 1, 0), 3), ((1, 2, 0), 3)]
     elif len(dims) == 2:
         wish = [((0, 1), 1), ((1, 0), 1)]
     else:
@@ -37,6 +37,13 @@
     return streams
 
 
+def turns(dims, n_streams):
+    if ORDER is not None and len(dims) == 3:
+        return ORDER
+    steps = 2 + 2 * sum(1 if n == 2 else 2 * (n - 1) for n in dims)
+    return [j for _ in range(steps) for j in range(n_streams)]
+
+
 def phase_slots(n):
     return 1 if n == 2 else 2 * (n - 1)
 
@@ -134,7 +141,8 @@
                             remote(mine(s), slot(side, k), sems[side][k], a,
                                    1 - 2 * side).wait_send()
                     ends.append(end)
-                yield
+                    if n > 2 or side == 1:
+                        yield
             for side in range(2):
                 @pl.when((p if side == 0 else n - 1 - p) > 0)
                 def _():
@@ -183,23 +191,23 @@
                                 block = block_of(s)
                                 remote(block, block, sems[side][k], a, step).wait_send()
                         ends.append(end)
-                if k < n - 1:
-                    yield
+                        if n > 2 or side == 1:
+                            yield
         store = pltpu.make_async_copy(gath.at[rows], out_hbm.at[rows], out_sem.at[2 * j + 1])
         store.start()
         ends.append(store.wait)
 
     running = [stream(j) for j in range(len(streams))]
-    first = True
-    while running:
-        for one in list(running):
-            if next(one, "end") == "end":
-                running.remove(one)
-            elif first:
-                first = False
-                peers = sum((pos[a] < dims[a] - 1).astype(jnp.int32)
-                            + (pos[a] > 0).astype(jnp.int32) for a in axes)
-                pl.semaphore_wait(barrier, peers)
+    greeted = False
+    began = set()
+    for j in turns(dims, len(streams)):
+        if j in began and not greeted:
+            greeted = True
+            peers = sum((pos[a] < dims[a] - 1).astype(jnp.int32)
+                        + (pos[a] > 0).astype(jnp.int32) for a in axes)
+            pl.semaphore_wait(barrier, peers)
+        began.add(j)
+        next(running[j], None)
     for end in ends:
         end()
 
@@ -235,7 +243,7 @@
     new_global, new_momentum = pl.pallas_call(
         functools.partial(kernel, dims, streams, n_sems),
         out_shape=(jax.ShapeDtypeStruct(wide, f32), jax.ShapeDtypeStruct(narrow, f32)),
-        in_specs=[pl.BlockSpec(memory_space=pl.ANY)] * 3,
+        in_specs=[pl.BlockSpec(memory_space=pltpu.HBM)] * 3,
         out_specs=(pl.BlockSpec(memory_space=pl.ANY),) * 2,
         scratch_shapes=[
             pltpu.VMEM(wide, f32), pltpu.VMEM(wide, f32), pltpu.VMEM(narrow, f32),

time: 92.1 us -> 87.6 us (0.951)
  Pallas kernels: 83.2 us -> 78.7 us
    pallas_call x1, Pallas kernels: 83.2 us -> 78.7 us  [body(): pl.pallas_call(functools.partial(kernel, dims, streams, n_sems), out_shap...]
where the time goes in v2:
time: 87.6 us; the launch traced here: 87.4 us
  Pallas kernels  78.7 us (90%)
  local copies, waits for them, and re-layouts  8.04 us (9%)
    pallas_call x1, Pallas kernels, body(): pl.pallas_call(functools.partial(kernel, dims, streams, n_sems), out_shap...  78.7 us
    unnamed x8, local copies, waits for them, and re-layouts  8.04 us

profile of v2, /device:TPU:0, one launch (start us, length us, event | category | flops | bytes accessed | tf_op | source)
XLA Modules:
  0.0 87.4 jit_solution(1330266570008623650)
XLA Ops:
  0.6 0.0 copy-start
  0.6 2.2 %copy-done = f32[4,32,8192]{2,1,0:T(8,128)S(1)} copy-done((f32[4,32,8192]{2,1,0:T(8,128)S(1)}, f32[4,32,8192]{2,1,0:T(8,128)}, u32[]{:S(2)}) %copy-start) | copy-done | bytes 4194328
  2.8 0.0 copy-start.1
  2.8 2.2 %copy-done.1 = f32[1,4,32,8192]{3,2,1,0:T(8,128)S(1)} copy-done((f32[1,4,32,8192]{3,2,1,0:T(8,128)S(1)}, f32[1,4,32,8192]{3,2,1,0:T(8,128)}, u32[]{:S(2)}) %copy-start.1) | copy-done | bytes 4194328
  5.0 0.0 copy-start.2
  5.0 0.9 %copy-done.2 = f32[4,32,512]{2,1,0:T(8,128)S(1)} copy-done((f32[4,32,512]{2,1,0:T(8,128)S(1)}, f32[4,32,512]{2,1,0:T(8,128)}, u32[]{:S(2)}) %copy-start.2) | copy-done | bytes 262168
  6.0 78.7 %shard_map.50 = (f32[16,4,2,2,4,8,128]{6,5,4,3,2,1,0:T(8,128)S(1)}, f32[16,4,8,128]{3,2,1,0:T(8,128)S(1)}) custom-call(f32[16,4,2,2,4,8,128]{6,5,4,3,2,1,0:T(8,128)S(1)} %bitcast.21, f32[16,4,2,2,4,8,128]{6,5,4,3,2,1,0:T(8,128)S(1)} %bitcast.22, f32[16,4,8,128]{3,2,1,0:T(8,128)S(1)} %bitcast.24), custom_call_target="tpu_custom_call" | custom-call | tf_op jit(solution)/shard_map/pallas_call | solution.py:243
  84.7 2.0 %copy.7 = f32[4,32,8192]{2,1,0:T(8,128)} copy(f32[4,32,8192]{2,1,0:T(8,128)S(1)} %bitcast.23) | data formatting | bytes 8388608
  86.7 0.7 copy.8
Async XLA Ops:
  0.6 2.2 %copy-start = (f32[4,32,8192]{2,1,0:T(8,128)S(1)}, f32[4,32,8192]{2,1,0:T(8,128)}, u32[]{:S(2)}) copy-start(f32[4,32,8192]{2,1,0:T(8,128)} %param.3) | copy-start | bytes 12582916
  2.8 2.2 %copy-start.1 = (f32[1,4,32,8192]{3,2,1,0:T(8,128)S(1)}, f32[1,4,32,8192]{3,2,1,0:T(8,128)}, u32[]{:S(2)}) copy-start(f32[1,4,32,8192]{3,2,1,0:T(8,128)} %param.4) | copy-start | bytes 12582916
  5.0 0.9 %copy-start.2 = (f32[4,32,512]{2,1,0:T(8,128)S(1)}, f32[4,32,512]{2,1,0:T(8,128)}, u32[]{:S(2)}) copy-start(f32[4,32,512]{2,1,0:T(8,128)} %param.5) | copy-start | bytes 786436

commit v3 on v2

--- a/solution.py
+++ b/solution.py
@@ -9,7 +9,7 @@
 
 NESTEROV = 0.9
 OUTER_RATE = 0.7
-ORDER = [2, 2, 1, 1, 0, 3, 3, 5, 3, 0, 3, 0, 4, 0, 3, 2, 1, 5, 3, 4, 3, 0, 0, 2, 1, 2, 0, 3, 2, 1, 1, 2, 0, 1, 2, 2, 4, 5, 1, 1, 2, 2, 1, 1, 2, 2, 1, 0, 1, 4, 2, 5, 2, 4, 5, 3, 1, 1, 0, 4, 3, 2, 4, 1, 5, 5, 4, 4, 5, 5, 0, 3, 4, 4, 5, 5, 4, 1, 2, 4, 5, 4, 5, 3, 3, 5, 5, 0, 3, 5, 4, 4, 0, 3, 1, 3, 3, 5, 4, 0, 0, 0, 0, 2, 0, 3, 5, 4]
+ORDER = [2, 2, 6, 6, 0, 0, 1, 4, 1, 0, 5, 3, 0, 0, 3, 5, 7, 3, 6, 0, 3, 2, 7, 3, 5, 0, 6, 6, 4, 1, 3, 6, 6, 3, 2, 5, 5, 6, 2, 2, 7, 6, 5, 5, 0, 1, 1, 4, 2, 5, 6, 6, 2, 3, 5, 7, 1, 2, 7, 6, 6, 0, 5, 5, 3, 2, 4, 1, 4, 7, 7, 6, 0, 5, 5, 6, 1, 1, 4, 4, 0, 3, 5, 5, 2, 7, 1, 1, 4, 2, 6, 5, 4, 0, 7, 1, 2, 4, 1, 4, 2, 3, 7, 7, 5, 2, 0, 6, 1, 4, 1, 2, 7, 4, 7, 4, 1, 7, 0, 7, 3, 7, 4, 3, 4, 6, 2, 0, 1, 0, 4, 3, 3, 0, 5, 7, 3, 3, 1, 0, 3, 2, 4, 7]
 LANES = 128
 SUBLANES = 8
 
@@ -21,7 +21,7 @@
 def plan(dims, groups):
     if len(dims) == 3:
         z, y, x = 0, 1, 2
-        wish = [((0, 1, 2), 2), ((2, 1, 0), 3), ((1, 2, 0), 3), ((0, 2, 1), 2), ((2, 1, 0), 3), ((1, 2, 0), 3)]
+        wish = [((0, 1, 2), 2), ((2, 1, 0), 2), ((1, 2, 0), 2), ((0, 2, 1), 2), ((2, 1, 0), 2), ((1, 2, 0), 2), ((2, 1, 0), 2), ((1, 2, 0), 2)]
     elif len(dims) == 2:
         wish = [((0, 1), 1), ((1, 0), 1)]
     else:

time: 87.6 us -> 83.8 us (0.957)
  Pallas kernels: 78.7 us -> 74.9 us
    pallas_call x1, Pallas kernels: 78.7 us -> 74.9 us  [body(): pl.pallas_call(functools.partial(kernel, dims, streams, n_sems), out_shap...]
where the time goes in v3:
time: 83.8 us; the launch traced here: 83.6 us
  Pallas kernels  74.9 us (89%)
  local copies, waits for them, and re-layouts  8.04 us (10%)
    pallas_call x1, Pallas kernels, body(): pl.pallas_call(functools.partial(kernel, dims, streams, n_sems), out_shap...  74.9 us
    unnamed x8, local copies, waits for them, and re-layouts  8.04 us

profile of v3, /device:TPU:0, one launch (start us, length us, event | category | flops | bytes accessed | tf_op | source)
XLA Modules:
  0.0 83.6 jit_solution(8063644003795608066)
XLA Ops:
  0.6 0.0 copy-start
  0.6 2.2 %copy-done = f32[4,32,8192]{2,1,0:T(8,128)S(1)} copy-done((f32[4,32,8192]{2,1,0:T(8,128)S(1)}, f32[4,32,8192]{2,1,0:T(8,128)}, u32[]{:S(2)}) %copy-start) | copy-done | bytes 4194328
  2.8 0.0 copy-start.1
  2.8 2.2 %copy-done.1 = f32[1,4,32,8192]{3,2,1,0:T(8,128)S(1)} copy-done((f32[1,4,32,8192]{3,2,1,0:T(8,128)S(1)}, f32[1,4,32,8192]{3,2,1,0:T(8,128)}, u32[]{:S(2)}) %copy-start.1) | copy-done | bytes 4194328
  5.0 0.0 copy-start.2
  5.0 0.9 %copy-done.2 = f32[4,32,512]{2,1,0:T(8,128)S(1)} copy-done((f32[4,32,512]{2,1,0:T(8,128)S(1)}, f32[4,32,512]{2,1,0:T(8,128)}, u32[]{:S(2)}) %copy-start.2) | copy-done | bytes 262168
  6.0 74.9 %shard_map.50 = (f32[16,4,2,2,4,8,128]{6,5,4,3,2,1,0:T(8,128)S(1)}, f32[16,4,8,128]{3,2,1,0:T(8,128)S(1)}) custom-call(f32[16,4,2,2,4,8,128]{6,5,4,3,2,1,0:T(8,128)S(1)} %bitcast.21, f32[16,4,2,2,4,8,128]{6,5,4,3,2,1,0:T(8,128)S(1)} %bitcast.22, f32[16,4,8,128]{3,2,1,0:T(8,128)S(1)} %bitcast.24), custom_call_target="tpu_custom_call" | custom-call | tf_op jit(solution)/shard_map/pallas_call | solution.py:243
  80.8 2.0 %copy.7 = f32[4,32,8192]{2,1,0:T(8,128)} copy(f32[4,32,8192]{2,1,0:T(8,128)S(1)} %bitcast.23) | data formatting | bytes 8388608
  82.9 0.7 copy.8
Async XLA Ops:
  0.6 2.2 %copy-start = (f32[4,32,8192]{2,1,0:T(8,128)S(1)}, f32[4,32,8192]{2,1,0:T(8,128)}, u32[]{:S(2)}) copy-start(f32[4,32,8192]{2,1,0:T(8,128)} %param.3) | copy-start | bytes 12582916
  2.8 2.2 %copy-start.1 = (f32[1,4,32,8192]{3,2,1,0:T(8,128)S(1)}, f32[1,4,32,8192]{3,2,1,0:T(8,128)}, u32[]{:S(2)}) copy-start(f32[1,4,32,8192]{3,2,1,0:T(8,128)} %param.4) | copy-start | bytes 12582916
  5.0 0.9 %copy-start.2 = (f32[4,32,512]{2,1,0:T(8,128)S(1)}, f32[4,32,512]{2,1,0:T(8,128)}, u32[]{:S(2)}) copy-start(f32[4,32,512]{2,1,0:T(8,128)} %param.5) | copy-start | bytes 786436

commit v4 on v3

--- a/solution.py
+++ b/solution.py
@@ -48,8 +48,8 @@
     return 1 if n == 2 else 2 * (n - 1)
 
 
-def kernel(dims, streams, n_sems, g_hbm, l_hbm, m_hbm, out_hbm, nm_hbm,
-           gw, lw, mom, acc, gath, nm, landing, send_sem, recv_sem, in_sem, out_sem):
+def kernel(dims, streams, n_sems, gw, lw, mom, out_hbm, nm_hbm,
+           acc, gath, nm, landing, send_sem, recv_sem, out_sem):
     axes = range(len(dims))
     me = lax.axis_index("island")
     strides = []
@@ -61,19 +61,6 @@
     pos = [(me // strides[a]) % dims[a] for a in axes]
     islands = strides[0] * dims[0]
 
-    loads = []
-    for j, (_, g0, ng) in enumerate(streams):
-        rows = pl.ds(g0, ng)
-        loads.append([
-            pltpu.make_async_copy(g_hbm.at[rows], gw.at[rows], in_sem.at[3 * j]),
-            pltpu.make_async_copy(l_hbm.at[rows], lw.at[rows], in_sem.at[3 * j + 1]),
-            pltpu.make_async_copy(m_hbm.at[rows], mom.at[rows], in_sem.at[3 * j + 2]),
-        ])
-        for load in loads[-1][:2]:
-            load.start()
-    for load in loads:
-        load[2].start()
-
     barrier = pltpu.get_barrier_semaphore()
     for a in axes:
         for step, there in ((1, pos[a] < dims[a] - 1), (-1, pos[a] > 0)):
@@ -99,8 +86,6 @@
     def stream(j):
         order, g0, ng = streams[j]
         rows = pl.ds(g0, ng)
-        loads[j][0].wait()
-        loads[j][1].wait()
         acc[rows] = gw[rows] - lw[rows]
         yield
         fixed = {}
@@ -150,7 +135,6 @@
             fixed[a] = p
 
         own = (rows,) + tuple(pos)
-        loads[j][2].wait()
         outer = acc[own] / islands
         moment = NESTEROV * mom[rows] + outer
         nm[rows] = moment
@@ -243,14 +227,12 @@
     new_global, new_momentum = pl.pallas_call(
         functools.partial(kernel, dims, streams, n_sems),
         out_shape=(jax.ShapeDtypeStruct(wide, f32), jax.ShapeDtypeStruct(narrow, f32)),
-        in_specs=[pl.BlockSpec(memory_space=pltpu.HBM)] * 3,
+        in_specs=[pl.BlockSpec(memory_space=pltpu.VMEM)] * 3,
         out_specs=(pl.BlockSpec(memory_space=pl.ANY),) * 2,
         scratch_shapes=[
             pltpu.VMEM(wide, f32), pltpu.VMEM(wide, f32), pltpu.VMEM(narrow, f32),
-            pltpu.VMEM(wide, f32), pltpu.VMEM(wide, f32), pltpu.VMEM(narrow, f32),
             landings,
             pltpu.SemaphoreType.DMA((n_sems,)), pltpu.SemaphoreType.DMA((n_sems,)),
-            pltpu.SemaphoreType.DMA((3 * len(streams),)),
             pltpu.SemaphoreType.DMA((2 * len(streams),)),
         ],
         compiler_params=pltpu.CompilerParams(

time: 83.8 us -> 82.6 us (0.986)
  Pallas kernels: 74.9 us -> 73.7 us
    pallas_call x1, Pallas kernels: 74.9 us -> 73.7 us  [body(): pl.pallas_call(functools.partial(kernel, dims, streams, n_sems), out_shap...]
where the time goes in v4:
time: 82.6 us; the launch traced here: 82.4 us
  Pallas kernels  73.7 us (89%)
  local copies, waits for them, and re-layouts  8.04 us (10%)
    pallas_call x1, Pallas kernels, body(): pl.pallas_call(functools.partial(kernel, dims, streams, n_sems), out_shap...  73.7 us
    unnamed x8, local copies, waits for them, and re-layouts  8.04 us

profile of v4, /device:TPU:0, one launch (start us, length us, event | category | flops | bytes accessed | tf_op | source)
XLA Modules:
  0.0 82.4 jit_solution(8351114231505004173)
XLA Ops:
  0.6 0.0 copy-start
  0.6 2.2 %copy-done = f32[4,32,8192]{2,1,0:T(8,128)S(1)} copy-done((f32[4,32,8192]{2,1,0:T(8,128)S(1)}, f32[4,32,8192]{2,1,0:T(8,128)}, u32[]{:S(2)}) %copy-start) | copy-done | bytes 4194328
  2.8 0.0 copy-start.1
  2.8 2.2 %copy-done.1 = f32[1,4,32,8192]{3,2,1,0:T(8,128)S(1)} copy-done((f32[1,4,32,8192]{3,2,1,0:T(8,128)S(1)}, f32[1,4,32,8192]{3,2,1,0:T(8,128)}, u32[]{:S(2)}) %copy-start.1) | copy-done | bytes 4194328
  5.0 0.0 copy-start.2
  5.0 0.9 %copy-done.2 = f32[4,32,512]{2,1,0:T(8,128)S(1)} copy-done((f32[4,32,512]{2,1,0:T(8,128)S(1)}, f32[4,32,512]{2,1,0:T(8,128)}, u32[]{:S(2)}) %copy-start.2) | copy-done | bytes 262168
  6.0 73.7 %shard_map.50 = (f32[16,4,2,2,4,8,128]{6,5,4,3,2,1,0:T(8,128)S(1)}, f32[16,4,8,128]{3,2,1,0:T(8,128)S(1)}) custom-call(f32[16,4,2,2,4,8,128]{6,5,4,3,2,1,0:T(8,128)S(1)} %bitcast.21, f32[16,4,2,2,4,8,128]{6,5,4,3,2,1,0:T(8,128)S(1)} %bitcast.22, f32[16,4,8,128]{3,2,1,0:T(8,128)S(1)} %bitcast.24), custom_call_target="tpu_custom_call" | custom-call | tf_op jit(solution)/shard_map/pallas_call | solution.py:227
  79.7 2.0 %copy.7 = f32[4,32,8192]{2,1,0:T(8,128)} copy(f32[4,32,8192]{2,1,0:T(8,128)S(1)} %bitcast.23) | data formatting | bytes 8388608
  81.7 0.7 copy.8
Async XLA Ops:
  0.6 2.2 %copy-start = (f32[4,32,8192]{2,1,0:T(8,128)S(1)}, f32[4,32,8192]{2,1,0:T(8,128)}, u32[]{:S(2)}) copy-start(f32[4,32,8192]{2,1,0:T(8,128)} %param.3) | copy-start | bytes 12582916
  2.8 2.2 %copy-start.1 = (f32[1,4,32,8192]{3,2,1,0:T(8,128)S(1)}, f32[1,4,32,8192]{3,2,1,0:T(8,128)}, u32[]{:S(2)}) copy-start(f32[1,4,32,8192]{3,2,1,0:T(8,128)} %param.4) | copy-start | bytes 12582916
  5.0 0.9 %copy-start.2 = (f32[4,32,512]{2,1,0:T(8,128)S(1)}, f32[4,32,512]{2,1,0:T(8,128)}, u32[]{:S(2)}) copy-start(f32[4,32,512]{2,1,0:T(8,128)} %param.5) | copy-start | bytes 786436
